TPU v7x, 32 devices: a whole 2x2x4 slice. The times are simulated.
32 devices in a mesh: segment: 2 (over y), fsdp: 4 (over x, core), seq: 4 (over z).
Axes of the slice: x: 2, y: 2, z: 4, core: 2. Of those that a mesh axis runs over, the one named last changes fastest.
Arguments:
- arriving: bfloat16 [2, 4, 768, 2048], P('segment', 'fsdp', 'seq'), may hold values from -6 to 6
- gain: float32 [2, 2048], P('segment'), may hold values from 0.1 to 1.9
- input_weight: bfloat16 [2, 2048, 16, 3, 128], P('segment', 'fsdp', 'seq')
- output_weight: bfloat16 [2, 16, 128, 2048], P('segment', 'seq', None, 'fsdp'), may hold values from -1 to 1
- block_pattern: int32 [2, 4, 24, 6], P('segment', 'fsdp'), may hold values from 0 to 23, as said below
Outputs:
- passed: bfloat16 [2, 4, 768, 2048], P('segment', 'fsdp', 'seq')
Inputs may be any that keep to these rules, and one draw needn't show every extreme that they name: `block_pattern`: row j of a document lists 6 different blocks; the first three are j - 1, j and j + 1 modulo 24, and block 0 is listed in every row.
All inputs are finite; a program needn't handle non-finite values.
Results may differ from a plain program's by a relative error of at most 0.012.
Values may be sent and summed in bfloat16 or wider, within the bound.
A program may use at most 64 MiB of HBM per device.

v0:
```python
import jax
import jax.numpy as jnp
from jax import lax
from jax.sharding import PartitionSpec as P

BLOCK = 32
SEL = 6
EPSILON = 1e-05


def passed_along(value, axis, steps):
    count = lax.axis_size(axis)
    pairs = [(source, (source + steps) % count) for source in range(count)]
    return lax.ppermute(value, axis, pairs)


def normalize(tokens, gain_row):
    values = tokens.astype(jnp.float32)
    spread = jnp.mean(values * values, axis=-1, keepdims=True)
    return (values * lax.rsqrt(spread + EPSILON) * gain_row).astype(jnp.bfloat16)


def attend(projected, pattern_rows):
    length, head_group, triple, head_width = projected.shape
    block_count = length // BLOCK
    query_rows = projected[:, :, 0].reshape(block_count, BLOCK, head_group, head_width)
    key_blocks = projected[:, :, 1].reshape(block_count, BLOCK, head_group, head_width)
    value_blocks = projected[:, :, 2].reshape(block_count, BLOCK, head_group, head_width)
    key_rows = jnp.take(key_blocks, pattern_rows, axis=0).reshape(
        block_count, SEL * BLOCK, head_group, head_width
    )
    value_rows = jnp.take(value_blocks, pattern_rows, axis=0).reshape(
        block_count, SEL * BLOCK, head_group, head_width
    )
    scores = jnp.einsum(
        "qbge,qnge->gqbn", query_rows, key_rows, preferred_element_type=jnp.float32
    ) * head_width ** (-0.5)
    row_max = jnp.max(scores, axis=-1, keepdims=True)
    exponent = jnp.exp(scores - row_max)
    weights = (exponent / jnp.sum(exponent, axis=-1, keepdims=True)).astype(jnp.bfloat16)
    mixed_rows = jnp.einsum(
        "gqbn,qnge->qbge", weights, value_rows, preferred_element_type=jnp.float32
    )
    return mixed_rows.astype(jnp.bfloat16).reshape(length, head_group * head_width)


def body(arriving, gain, input_weight, output_weight, block_pattern):
    tokens = arriving[0, 0]
    row_count = tokens.shape[0]
    normed = normalize(tokens, gain[0])
    slab_rows, head_group, triple, head_size = input_weight.shape[1:]
    columns = head_group * triple * head_size
    panel_flat = input_weight[0].reshape(slab_rows, columns)
    length = row_count * lax.axis_size("seq")
    whole_panel = lax.all_gather(panel_flat, "fsdp", axis=0, tiled=True)
    projected = jnp.dot(
        lax.all_gather(normed, "seq", axis=0, tiled=True),
        whole_panel,
        preferred_element_type=jnp.float32,
    )
    projected = projected.astype(jnp.bfloat16).reshape(length, head_group, triple, head_size)
    mixed_rows = attend(projected, block_pattern[0, 0])
    out_panel = output_weight[0].reshape(head_group * head_size, -1)
    whole_out = lax.all_gather(out_panel, "fsdp", axis=1, tiled=True)
    branch = lax.psum_scatter(
        jnp.dot(mixed_rows, whole_out, preferred_element_type=jnp.float32).astype(jnp.bfloat16),
        "seq",
        scatter_dimension=0,
        tiled=True,
    ).astype(jnp.float32)
    updated = (tokens.astype(jnp.float32) + branch).astype(jnp.bfloat16)
    passed = passed_along(updated, "segment", 1)
    return passed[None, None]


def solution(mesh):
    in_specs = (
        P("segment", "fsdp", "seq", None),
        P("segment", None),
        P("segment", "fsdp", "seq", None, None),
        P("segment", "seq", None, "fsdp"),
        P("segment", "fsdp", None, None),
    )
    out_specs = P("segment", "fsdp", "seq", None)
    return jax.shard_map(body, mesh=mesh, in_specs=in_specs, out_specs=out_specs, check_vma=False)
```

profile of v0, /device:TPU:0, one launch (start us, length us, event | category | flops | bytes accessed | tf_op | source)
XLA Modules:
  0.0 277.0 jit_solution(2608817675597869169)
XLA Ops:
  6.5 0.0 copy-start.1
  6.5 0.0 all-gather.4.cloned.1.call-start
  6.5 1.5 fusion.4
  8.0 2.3 fusion.6
  10.3 0.0 copy-start.2
  10.3 0.0 all-gather.4.cloned.1.call-update
  10.3 0.0 all-gather.6.cloned.1.call-start
  10.4 0.0 copy-done.1
  10.4 2.6 copy.24
  13.0 0.0 all-gather.6.cloned.1.call-update
  13.0 0.0 all-gather.8.cloned.1.call-start
  13.0 0.7 all-gather.8.cloned.1.call-update
  13.7 0.0 reduce-scatter.2.cloned.1.call-start
  13.8 0.0 copy-done.2
  13.8 0.1 copy.27
  13.9 0.1 reshape.54
  14.0 0.1 copy.23
  14.1 62.6 %all-gather.4.cloned.1.call-done = bf16[768,2048]{1,0:T(8,128)(2,1)} async-done(((bf16[192,2048]{1,0:T(8,128)(2,1)}), bf16[768,2048]{1,0:T(8,128)(2,1)}) %all-gather.4.cloned.1.call-update) | async-done | bytes 3145744 | tf_op jit(solution)/shard_map/all_gather | solution.py:57
  76.7 46.6 %all-gather.6.cloned.1.call-done = bf16[2048,1536]{0,1:T(8,128)(2,1)} async-done(((bf16[512,1536]{0,1:T(8,128)(2,1)}), bf16[2048,1536]{0,1:T(8,128)(2,1)}) %all-gather.6.cloned.1.call-update) | async-done | bytes 6291472 | tf_op jit(solution)/shard_map/all_gather | solution.py:55
  123.3 9.3 %convolution_convert_fusion.1 = bf16[768,1536]{1,0:T(8,128)(2,1)} fusion(bf16[768,2048]{1,0:T(8,128)(2,1)} %all-gather.4.cloned.1.call-done, bf16[2048,1536]{0,1:T(8,128)(2,1)} %all-gather.6.cloned.1.call-done), kind=kOutput, calls=%fused_computation.6 | convolution fusion | flops 4833017856 | bytes 11796480 | tf_op jit(solution)/shard_map/dot_general | solution.py:56
  132.6 2.9 %copy.25 = bf16[768,1536]{0,1:T(8,128)(2,1)S(1)} copy(bf16[768,1536]{1,0:T(8,128)(2,1)} %convolution_convert_fusion.1) | data formatting | bytes 4718592 | tf_op jit(solution)/shard_map/convert_element_type | solution.py:61
  135.5 1.3 fusion.20
  136.8 1.5 copy.31
  138.3 1.5 copy.26
  139.8 7.6 %gather_fusion.1 = bf16[144,32,4,128]{3,1,2,0:T(8,128)(2,1)} fusion(bf16[24,32,4,128]{3,1,0,2:T(8,128)(2,1)S(1)} %bitcast.37, s32[1024]{0:T(1024)S(1)} %pad_clamp_fusion), kind=kCustom, calls=%fused_computation.1.clone | custom fusion | bytes 9437760 | tf_op jit(solution)/shard_map/jit(_take)/gather | solution.py:29
  147.4 7.6 %gather_fusion = bf16[144,32,4,128]{3,1,2,0:T(8,128)(2,1)} fusion(bf16[24,32,4,128]{3,1,0,2:T(8,128)(2,1)S(1)} %bitcast.36, s32[1024]{0:T(1024)S(1)} %pad_clamp_fusion), kind=kCustom, calls=%fused_computation.clone | custom fusion | bytes 9437760 | tf_op jit(solution)/shard_map/jit(_take)/gather | solution.py:32
  155.0 5.7 %broadcast_select_fusion = (bf16[24,6,32,4,128]{4,2,3,1,0:T(8,128)(2,1)S(1)}, bf16[24,6,32,4,128]{4,2,3,1,0:T(8,128)(2,1)}) fusion(bf16[24,6,32,4,128]{4,2,3,1,0:T(8,128)(2,1)} %bitcast.38, pred[24,6]{1,0:T(8,128)(4,1)S(1)} %copy.23, bf16[24,6,32,4,128]{4,2,3,1,0:T(8,128)(2,1)} %bitcast.39), kind=kLoop, calls=%fused_computation.3 | loop fusion | flops 4718592 | bytes 18874512 | tf_op jit(solution)/shard_map/jit(_take)/select_n | solution.py:29
  160.7 3.6 %copy.33 = bf16[24,6,32,4,128]{4,2,1,0,3:T(8,128)(2,1)} copy(bf16[24,6,32,4,128]{4,2,3,1,0:T(8,128)(2,1)S(1)} %get-tuple-element.9) | data formatting | bytes 9437184 | tf_op jit(solution)/shard_map/jit(_take)/select_n | solution.py:29
  164.2 0.4 copy.29
  164.6 5.9 %copy.28 = bf16[24,6,32,4,128]{4,2,1,3,0:T(8,128)(2,1)} copy(bf16[24,6,32,4,128]{4,2,3,1,0:T(8,128)(2,1)} %get-tuple-element.10) | data formatting | bytes 9437184 | tf_op jit(solution)/shard_map/jit(_take)/select_n | solution.py:32
  170.5 7.2 %fusion.21 = (f32[4,24,32]{2,1,0:T(8,128)S(1)}, f32[4,24,32,192]{3,2,1,0:T(8,128)}) fusion(bf16[24,32,4,128]{3,1,0,2:T(8,128)(2,1)S(1)} %bitcast.44, bf16[24,192,4,128]{3,1,0,2:T(8,128)(2,1)} %bitcast.40), kind=kOutput, calls=%fused_computation.31 | convolution fusion | flops 152764608 | bytes 7876608 | tf_op jit(solution)/shard_map/sub | solution.py:39
  177.7 5.2 %fusion.14 = bf16[24,32,4,128]{3,1,2,0:T(8,128)(2,1)S(1)} fusion(bf16[24,192,4,128]{3,1,2,0:T(8,128)(2,1)} %bitcast.43, f32[4,24,32,192]{3,2,1,0:T(8,128)} %get-tuple-element.12, f32[4,24,32]{2,1,0:T(8,128)S(1)} %get-tuple-element.11), kind=kOutput, calls=%fused_computation.22 | convolution fusion | flops 152567808 | bytes 7876608 | tf_op jit(solution)/shard_map/gqbn,qnge->qbge/dot_general | solution.py:41
  182.9 0.4 copy.35
  183.3 0.0 all-gather.8.cloned.1.call-done
  183.3 5.0 %convolution_convert_fusion = bf16[768,2048]{1,0:T(8,128)(2,1)} fusion(bf16[512,2048]{1,0:T(8,128)(2,1)} %all-gather.8.cloned.1.call-done, bf16[96,8,4,128]{3,2,1,0:T(4,128)(2,1)S(1)} %bitcast.45), kind=kOutput, calls=%fused_computation.5 | convolution fusion | flops 1612185600 | bytes 6029312 | tf_op jit(solution)/shard_map/dot_general | solution.py:66
  188.3 0.0 copy-start
  188.3 0.0 reduce-scatter.2.cloned.1.call-update
  188.4 60.6 %reduce-scatter.2.cloned.1.call-done = bf16[192,2048]{1,0:T(8,128)(2,1)} async-done(((bf16[768,2048]{1,0:T(8,128)(2,1)}), bf16[192,2048]{1,0:T(8,128)(2,1)}) %reduce-scatter.2.cloned.1.call-update) | async-done | bytes 786448 | tf_op jit(solution)/shard_map/reduce_scatter | solution.py:65
  248.9 0.0 copy-done
  248.9 1.4 fusion.7
  250.4 1.5 collective-permute-start
  251.9 17.7 %collective-permute-done = bf16[192,2048]{1,0:T(8,128)(2,1)S(1)} collective-permute-done((bf16[192,2048]{1,0:T(8,128)(2,1)S(1)}, bf16[192,2048]{1,0:T(8,128)(2,1)S(1)}, u32[]{:S(2)}, u32[]{:S(2)}) %collective-permute-start) | collective-permute-done | bytes 786464 | tf_op jit(solution)/shard_map/ppermute | solution.py:14
  269.5 0.9 copy.52
  (4 shorter events, 0.0 us)
Async XLA Ops:
  6.5 3.8 %copy-start.1 = (bf16[1,512,4,3,128]{4,2,3,1,0:T(4,128)(2,1)S(1)}, bf16[1,512,4,3,128]{4,2,3,1,0:T(4,128)(2,1)}, u32[]{:S(2)}) copy-start(bf16[1,512,4,3,128]{4,2,3,1,0:T(4,128)(2,1)} %param.9) | copy-start | bytes 4718596
  6.5 70.1 %all-gather.4.cloned.1.call-start = ((), (), s32[]{:S(2)}) async-start(), calls=%async_computation.1 | async-start | bytes 3932160 | tf_op jit(solution)/shard_map/all_gather | solution.py:57
  10.3 3.5 %copy-start.2 = (s32[1,1,24,6]{2,1,3,0:T(1,128)S(1)}, s32[1,1,24,6]{2,1,3,0:T(1,128)}, u32[]{:S(2)}) copy-start(s32[1,1,24,6]{2,1,3,0:T(1,128)} %param.11) | copy-start | bytes 1732
  10.3 113.0 %all-gather.6.cloned.1.call-start = ((), (), s32[]{:S(2)}) async-start(), calls=%async_computation.2 | async-start | bytes 7864320 | tf_op jit(solution)/shard_map/all_gather | solution.py:55
  13.0 170.3 %all-gather.8.cloned.1.call-start = ((), (), s32[]{:S(2)}) async-start(), calls=%async_computation.3 | async-start | bytes 2621440 | tf_op jit(solution)/shard_map/all_gather | solution.py:64
  13.7 235.2 %reduce-scatter.2.cloned.1.call-start = ((), (), s32[]{:S(2)}) async-start(), calls=%async_computation.4 | async-start | bytes 3932160 | tf_op jit(solution)/shard_map/reduce_scatter | solution.py:65
  188.3 60.6 %copy-start = (bf16[1,1,192,2048]{3,2,1,0:T(8,128)(2,1)S(1)}, bf16[1,1,192,2048]{3,2,1,0:T(8,128)(2,1)}, u32[]{:S(2)}) copy-start(bf16[1,1,192,2048]{3,2,1,0:T(8,128)(2,1)} %param.7) | copy-start | bytes 2359300
  250.4 19.2 %collective-permute-start = (bf16[192,2048]{1,0:T(8,128)(2,1)S(1)}, bf16[192,2048]{1,0:T(8,128)(2,1)S(1)}, u32[]{:S(2)}, u32[]{:S(2)}) collective-permute-start(bf16[192,2048]{1,0:T(8,128)(2,1)S(1)} %fusion.7), channel_id=1, source_target_pairs={{0,16},{16,0},{1,17},{17,1},{2,18},{18,2},{3,19},{19,3},{4,20},{20... | collective-permute-start | bytes 2359304 | tf_op jit(solution)/shard_map/ppermute | solution.py:14
Sparse Core Ops, SparseCore 0:
  10.5 66.1 all-gather.3
  78.2 45.0 all-gather.5
  124.9 22.5 all-gather.7
  188.5 60.4 reduce-scatter.1
where the time goes:
time: 277 us
  waiting for transfers between devices  188 us (68%)
  local copies, waits for them, and re-layouts  36.4 us (13%)
  matrix products  26.7 us (10%)
  between operations  13.2 us (5%)
  other arithmetic  10.8 us (4%)
    all_gather x1, waiting for transfers between devices, body(): lax.all_gather(normed, 'seq', axis=0, tiled=True)  62.6 us
    reduce_scatter x1, waiting for transfers between devices, body(): lax.psum_scatter(jnp.dot(mixed_rows, whole_out, preferred_element_type=jn...  60.6 us
    all_gather x1, waiting for transfers between devices, body(): whole_panel = lax.all_gather(panel_flat, 'fsdp', axis=0, tiled=True)  46.6 us
    ppermute x1, waiting for transfers between devices, passed_along(): return lax.ppermute(value, axis, pairs)  17.7 us
    dot_general x1, matrix products, body(): jnp.dot(lax.all_gather(normed, 'seq', axis=0, tiled=True), whole_panel, p...  9.27 us
    gather x1, local copies, waits for them, and re-layouts, attend(): jnp.take(value_blocks, pattern_rows, axis=0)  7.62 us
    gather x1, local copies, waits for them, and re-layouts, attend(): jnp.take(key_blocks, pattern_rows, axis=0)  7.56 us
    sub x1, matrix products, attend(): exponent = jnp.exp(scores - row_max)  7.16 us
  transfers between devices with their start and end apart: 5, of which 4 were waited for; matrix products, arithmetic and copies ran while one was open for 23% of the time, Pallas kernels for 0%

commit v1 on v0

--- a/solution.py
+++ b/solution.py
@@ -52,7 +52,16 @@
     columns = head_group * triple * head_size
     panel_flat = input_weight[0].reshape(slab_rows, columns)
     length = row_count * lax.axis_size("seq")
-    whole_panel = lax.all_gather(panel_flat, "fsdp", axis=0, tiled=True)
+    side_arr, big = (jax.lax.axis_size("fsdp"), jax.lax.axis_index("fsdp"))
+    whole_panel, upper = (panel_flat, 1)
+    while upper < side_arr:
+        aux = jax.lax.ppermute(
+            whole_panel, "fsdp", [(dev_i, dev_i ^ upper) for dev_i in range(side_arr)]
+        )
+        next_value = jnp.concatenate([whole_panel, aux], axis=0)
+        oldest = jnp.concatenate([aux, whole_panel], axis=0)
+        whole_panel = jnp.where(big & upper == 0, next_value, oldest)
+        upper = 2 * upper
     projected = jnp.dot(
         lax.all_gather(normed, "seq", axis=0, tiled=True),
         whole_panel,

time: 277 us -> 251 us (0.906)
  waiting for transfers between devices: 188 us -> 155 us
  starting transfers between devices: 1.66 us -> 5 us
    ppermute x0 -> x2, waiting for transfers between devices: none -> 75 us  [body(): jax.lax.ppermute(whole_panel, 'fsdp', [(dev_i, dev_i ^ upper) for dev_i i...]
    all_gather x1, waiting for transfers between devices: 62.6 us -> 0.01 us  [body(): lax.all_gather(normed, 'seq', axis=0, tiled=True)]
    all_gather x1 -> x0, waiting for transfers between devices: 46.6 us -> none  [body(): whole_panel = lax.all_gather(panel_flat, 'fsdp', axis=0, tiled=True)]
    ppermute x0 -> x2, starting transfers between devices: none -> 3.38 us  [body(): jax.lax.ppermute(whole_panel, 'fsdp', [(dev_i, dev_i ^ upper) for dev_i i...]
  transfers between devices with their start and end apart: 5 -> 6, of which waited for: 4 -> 4; matrix products, arithmetic and copies ran while one was open for 23% -> 26% of each run, Pallas kernels for 0% -> 0%
where the time goes in v1:
time: 251 us; the launch traced here: 250 us
  waiting for transfers between devices  155 us (62%)
  local copies, waits for them, and re-layouts  35.2 us (14%)
  matrix products  28.6 us (11%)
  between operations  13.2 us (5%)
  other arithmetic  13 us (5%)
  starting transfers between devices  5 us (2%)
    ppermute x2, waiting for transfers between devices, body(): jax.lax.ppermute(whole_panel, 'fsdp', [(dev_i, dev_i ^ upper) for dev_i i...  75 us
    reduce_scatter x1, waiting for transfers between devices, body(): lax.psum_scatter(jnp.dot(mixed_rows, whole_out, preferred_element_type=jn...  62.7 us
    ppermute x1, waiting for transfers between devices, passed_along(): return lax.ppermute(value, axis, pairs)  17.6 us
    dot_general x1, matrix products, body(): jnp.dot(lax.all_gather(normed, 'seq', axis=0, tiled=True), whole_panel, p...  11.2 us
    gather x1, local copies, waits for them, and re-layouts, attend(): jnp.take(value_blocks, pattern_rows, axis=0)  7.62 us
    gather x1, local copies, waits for them, and re-layouts, attend(): jnp.take(key_blocks, pattern_rows, axis=0)  7.56 us
    sub x1, matrix products, attend(): exponent = jnp.exp(scores - row_max)  7.17 us
    select_n x2, local copies, waits for them, and re-layouts, attend(): jnp.take(value_blocks, pattern_rows, axis=0)  5.99 us
  transfers between devices with their start and end apart: 6, of which 4 were waited for; matrix products, arithmetic and copies ran while one was open for 26% of the time, Pallas kernels for 0%

profile of v1, /device:TPU:0, one launch (start us, length us, event | category | flops | bytes accessed | tf_op | source)
XLA Modules:
  0.0 250.4 jit_solution(10605426553385765655)
XLA Ops:
  6.5 0.0 copy-start.1
  6.5 0.0 all-gather.3.cloned.1.call-start
  6.5 1.5 fusion.12
  8.0 2.3 fusion.14
  10.3 0.0 all-gather.3.cloned.1.call-update
  10.3 0.0 all-gather.5.cloned.1.call-start
  10.4 0.0 copy-done.1
  10.4 1.4 copy.24
  11.8 0.5 collective-permute-start
  12.3 0.0 copy-start.2
  12.3 3.0 %collective-permute-done = bf16[512,1536]{0,1:T(8,128)(2,1)S(1)} collective-permute-done((bf16[512,1536]{0,1:T(8,128)(2,1)S(1)}, bf16[512,1536]{0,1:T(8,128)(2,1)S(1)}, u32[]{:S(2)}, u32[]{:S(2)}) %collective-permute-start) | collective-permute-done | bytes 1572896 | tf_op jit(solution)/shard_map/ppermute | solution.py:58
  15.4 2.2 maximum_select_fusion.4
  17.5 2.9 %collective-permute-start.1 = (bf16[1024,1536]{0,1:T(8,128)(2,1)}, bf16[1024,1536]{0,1:T(8,128)(2,1)}, u32[]{:S(2)}, u32[]{:S(2)}) collective-permute-start(bf16[1024,1536]{0,1:T(8,128)(2,1)} %maximum_select_fusion.4), channel_id=1, source_target_pairs={{0,8},{4,12},{8,0},{12,4},{1,9},{5,13},{9,1},{13,5},{2,10},{6,14},... | collective-permute-start | bytes 9437192 | tf_op jit(solution)/shard_map/ppermute | solution.py:58
  20.4 0.0 all-gather.5.cloned.1.call-update
  20.4 0.0 reduce-scatter.2.cloned.1.call-start
  20.5 0.0 copy-done.2
  20.5 0.1 copy.27
  20.6 0.1 reshape.54
  20.7 0.1 copy.23
  20.8 71.9 %collective-permute-done.1 = bf16[1024,1536]{0,1:T(8,128)(2,1)} collective-permute-done((bf16[1024,1536]{0,1:T(8,128)(2,1)}, bf16[1024,1536]{0,1:T(8,128)(2,1)}, u32[]{:S(2)}, u32[]{:S(2)}) %collective-permute-start.1) | collective-permute-done | bytes 3145760 | tf_op jit(solution)/shard_map/ppermute | solution.py:58
  92.7 0.0 all-gather.3.cloned.1.call-done
  92.7 11.2 %fusion.8 = bf16[768,1536]{1,0:T(8,128)(2,1)} fusion(bf16[768,2048]{1,0:T(8,128)(2,1)} %all-gather.3.cloned.1.call-done, bf16[1024,1536]{0,1:T(8,128)(2,1)} %collective-permute-done.1, bf16[1024,1536]{0,1:T(8,128)(2,1)} %maximum_select_fusion.4, pred[]{:T(512)S(6)} %eq.6), kind=kOutput, calls=%fused_computation.13 | convolution fusion | flops 4861329408 | bytes 11796481 | tf_op jit(solution)/shard_map/dot_general | solution.py:65
  103.9 2.8 %copy.25 = bf16[768,1536]{0,1:T(8,128)(2,1)S(1)} copy(bf16[768,1536]{1,0:T(8,128)(2,1)} %fusion.8) | data formatting | bytes 4718592 | tf_op jit(solution)/shard_map/convert_element_type | solution.py:70
  106.8 1.3 fusion.29
  108.1 1.5 copy.31
  109.6 1.5 copy.26
  111.1 7.6 %gather_fusion.1 = bf16[144,32,4,128]{3,1,2,0:T(8,128)(2,1)} fusion(bf16[24,32,4,128]{3,1,0,2:T(8,128)(2,1)S(1)} %bitcast.36, s32[1024]{0:T(1024)S(1)} %pad_clamp_fusion), kind=kCustom, calls=%fused_computation.1.clone | custom fusion | bytes 9437760 | tf_op jit(solution)/shard_map/jit(_take)/gather | solution.py:29
  118.7 7.6 %gather_fusion = bf16[144,32,4,128]{3,1,2,0:T(8,128)(2,1)} fusion(bf16[24,32,4,128]{3,1,0,2:T(8,128)(2,1)S(1)} %bitcast.35, s32[1024]{0:T(1024)S(1)} %pad_clamp_fusion), kind=kCustom, calls=%fused_computation.clone | custom fusion | bytes 9437760 | tf_op jit(solution)/shard_map/jit(_take)/gather | solution.py:32
  126.3 5.7 %broadcast_select_fusion = (bf16[24,6,32,4,128]{4,2,3,1,0:T(8,128)(2,1)S(1)}, bf16[24,6,32,4,128]{4,2,3,1,0:T(8,128)(2,1)}) fusion(bf16[24,6,32,4,128]{4,2,3,1,0:T(8,128)(2,1)} %bitcast.37, pred[24,6]{1,0:T(8,128)(4,1)S(1)} %copy.23, bf16[24,6,32,4,128]{4,2,3,1,0:T(8,128)(2,1)} %bitcast.38), kind=kLoop, calls=%fused_computation.11 | loop fusion | flops 4718592 | bytes 18874512 | tf_op jit(solution)/shard_map/jit(_take)/select_n | solution.py:29
  131.9 3.6 %copy.33 = bf16[24,6,32,4,128]{4,2,1,0,3:T(8,128)(2,1)} copy(bf16[24,6,32,4,128]{4,2,3,1,0:T(8,128)(2,1)S(1)} %get-tuple-element.9) | data formatting | bytes 9437184 | tf_op jit(solution)/shard_map/jit(_take)/select_n | solution.py:29
  135.5 0.4 copy.29
  135.9 5.9 %copy.28 = bf16[24,6,32,4,128]{4,2,1,3,0:T(8,128)(2,1)} copy(bf16[24,6,32,4,128]{4,2,3,1,0:T(8,128)(2,1)} %get-tuple-element.10) | data formatting | bytes 9437184 | tf_op jit(solution)/shard_map/jit(_take)/select_n | solution.py:32
  141.8 7.2 %fusion.30 = (f32[4,24,32]{2,1,0:T(8,128)S(1)}, f32[4,24,32,192]{3,2,1,0:T(8,128)}) fusion(bf16[24,32,4,128]{3,1,0,2:T(8,128)(2,1)S(1)} %bitcast.44, bf16[24,192,4,128]{3,1,0,2:T(8,128)(2,1)} %bitcast.39), kind=kOutput, calls=%fused_computation.41 | convolution fusion | flops 152764608 | bytes 7876608 | tf_op jit(solution)/shard_map/sub | solution.py:39
  149.0 5.2 %fusion.22 = bf16[24,32,4,128]{3,1,2,0:T(8,128)(2,1)S(1)} fusion(bf16[24,192,4,128]{3,1,2,0:T(8,128)(2,1)} %bitcast.43, f32[4,24,32,192]{3,2,1,0:T(8,128)} %get-tuple-element.12, f32[4,24,32]{2,1,0:T(8,128)S(1)} %get-tuple-element.11), kind=kOutput, calls=%fused_computation.31 | convolution fusion | flops 152567808 | bytes 7876608 | tf_op jit(solution)/shard_map/gqbn,qnge->qbge/dot_general | solution.py:41
  154.1 0.4 copy.35
  154.6 0.0 all-gather.5.cloned.1.call-done
  154.6 5.0 %convolution_convert_fusion = bf16[768,2048]{1,0:T(8,128)(2,1)} fusion(bf16[512,2048]{1,0:T(8,128)(2,1)} %all-gather.5.cloned.1.call-done, bf16[96,8,4,128]{3,2,1,0:T(4,128)(2,1)S(1)} %bitcast.45), kind=kOutput, calls=%fused_computation.14 | convolution fusion | flops 1612185600 | bytes 6029312 | tf_op jit(solution)/shard_map/dot_general | solution.py:75
  159.6 0.0 copy-start
  159.6 0.0 reduce-scatter.2.cloned.1.call-update
  159.7 62.7 %reduce-scatter.2.cloned.1.call-done = bf16[192,2048]{1,0:T(8,128)(2,1)} async-done(((bf16[768,2048]{1,0:T(8,128)(2,1)}), bf16[192,2048]{1,0:T(8,128)(2,1)}) %reduce-scatter.2.cloned.1.call-update) | async-done | bytes 786448 | tf_op jit(solution)/shard_map/reduce_scatter | solution.py:74
  222.4 0.0 copy-done
  222.4 1.4 fusion.15
  223.8 1.5 collective-permute-start.2
  225.3 17.6 %collective-permute-done.2 = bf16[192,2048]{1,0:T(8,128)(2,1)S(1)} collective-permute-done((bf16[192,2048]{1,0:T(8,128)(2,1)S(1)}, bf16[192,2048]{1,0:T(8,128)(2,1)S(1)}, u32[]{:S(2)}, u32[]{:S(2)}) %collective-permute-start.2) | collective-permute-done | bytes 786464 | tf_op jit(solution)/shard_map/ppermute | solution.py:14
  243.0 0.9 copy.52
  (4 shorter events, 0.0 us)
Async XLA Ops:
  6.5 3.8 %copy-start.1 = (bf16[1,512,4,3,128]{4,2,3,1,0:T(4,128)(2,1)S(1)}, bf16[1,512,4,3,128]{4,2,3,1,0:T(4,128)(2,1)}, u32[]{:S(2)}) copy-start(bf16[1,512,4,3,128]{4,2,3,1,0:T(4,128)(2,1)} %param.9) | copy-start | bytes 4718596
  6.5 86.2 %all-gather.3.cloned.1.call-start = ((), (), s32[]{:S(2)}) async-start(), calls=%async_computation.1 | async-start | bytes 3932160 | tf_op jit(solution)/shard_map/all_gather | solution.py:66
  10.3 144.3 %all-gather.5.cloned.1.call-start = ((), (), s32[]{:S(2)}) async-start(), calls=%async_computation.2 | async-start | bytes 2621440 | tf_op jit(solution)/shard_map/all_gather | solution.py:73
  11.8 3.6 %collective-permute-start = (bf16[512,1536]{0,1:T(8,128)(2,1)S(1)}, bf16[512,1536]{0,1:T(8,128)(2,1)S(1)}, u32[]{:S(2)}, u32[]{:S(2)}) collective-permute-start(bf16[512,1536]{0,1:T(8,128)(2,1)S(1)} %bitcast.41), channel_id=1, source_target_pairs={{0,4},{4,0},{8,12},{12,8},{1,5},{5,1},{9,13},{13,9},{2,6},{6,2},{1... | collective-permute-start | bytes 4718600 | tf_op jit(solution)/shard_map/ppermute | solution.py:58
  12.3 8.1 %copy-start.2 = (s32[1,1,24,6]{2,1,3,0:T(1,128)S(1)}, s32[1,1,24,6]{2,1,3,0:T(1,128)}, u32[]{:S(2)}) copy-start(s32[1,1,24,6]{2,1,3,0:T(1,128)} %param.11) | copy-start | bytes 1732
  17.5 75.2 %collective-permute-start.1 = (bf16[1024,1536]{0,1:T(8,128)(2,1)}, bf16[1024,1536]{0,1:T(8,128)(2,1)}, u32[]{:S(2)}, u32[]{:S(2)}) collective-permute-start(bf16[1024,1536]{0,1:T(8,128)(2,1)} %maximum_select_fusion.4), channel_id=1, source_target_pairs={{0,8},{4,12},{8,0},{12,4},{1,9},{5,13},{9,1},{13,5},{2,10},{6,14},... | collective-permute-start | bytes 9437192 | tf_op jit(solution)/shard_map/ppermute | solution.py:58
  20.4 202.0 %reduce-scatter.2.cloned.1.call-start = ((), (), s32[]{:S(2)}) async-start(), calls=%async_computation.3 | async-start | bytes 3932160 | tf_op jit(solution)/shard_map/reduce_scatter | solution.py:74
  159.6 62.8 %copy-start = (bf16[1,1,192,2048]{3,2,1,0:T(8,128)(2,1)S(1)}, bf16[1,1,192,2048]{3,2,1,0:T(8,128)(2,1)}, u32[]{:S(2)}) copy-start(bf16[1,1,192,2048]{3,2,1,0:T(8,128)(2,1)} %param.7) | copy-start | bytes 2359300
  223.8 19.2 %collective-permute-start.2 = (bf16[192,2048]{1,0:T(8,128)(2,1)S(1)}, bf16[192,2048]{1,0:T(8,128)(2,1)S(1)}, u32[]{:S(2)}, u32[]{:S(2)}) collective-permute-start(bf16[192,2048]{1,0:T(8,128)(2,1)S(1)} %fusion.15), channel_id=1, source_target_pairs={{0,16},{16,0},{1,17},{17,1},{2,18},{18,2},{3,19},{19,3},{4,20},{20... | collective-permute-start | bytes 2359304 | tf_op jit(solution)/shard_map/ppermute | solution.py:14
Sparse Core Ops, SparseCore 0:
  10.4 66.1 all-gather.2
  78.2 23.4 all-gather.4
  159.8 62.5 reduce-scatter.1
